TPU v7x, 32 devices: a whole 2x2x4 slice. The times are simulated.
32 devices in a mesh: grp: 4 (over z), blk: 8 (over y, x, core).
Axes of the slice: x: 2, y: 2, z: 4, core: 2. Of those that a mesh axis runs over, the one named last changes fastest.
Arguments:
- band_states: bfloat16 [64, 8, 1152], P(('grp', 'blk')), may hold values from -6 to 6
- kpoint_ids: int32 [64], P(('grp', 'blk')), may hold values from 0 to 2303, as said below
- screened: bfloat16 [2304, 1152], P('grp'), may hold values from 0.19921875 to 5
- coulomb: float32 [1152], replicated, may hold values from 0.2 to 5
- umklapp_map: int32 [4, 1152], replicated, may hold values from 0 to 1151, each once within a row
Outputs:
- kernel: float32 [64, 4, 512], P(('grp', 'blk'))
- mirror: float32 [64, 4, 512], P(('grp', 'blk'))
Inputs may be any that keep to these rules, and one draw needn't show every extreme that they name: `kpoint_ids`: 64 distinct flat indices row * 48 + col of the 48 x 48 grid, in increasing order along the k-points. `umklapp_map`: each row is a permutation of the 1152 G-vector indices.
All inputs are finite; a program needn't handle non-finite values.
Results may differ from a plain program's by a relative error of at most 0.011.
Values may be sent and summed in bfloat16 or wider, within the bound.
A program may use at most 128 MiB of HBM per device.

v0:
```python
import functools
import math

import jax
import jax.numpy as jnp
import ml_dtypes
import numpy as np
from jax import lax
from jax.experimental import pallas as pl
from jax.experimental.pallas import tpu as pltpu
from jax.sharding import PartitionSpec as P

NKX = 48
NKY = 48
NV = 4
NC = 4
STEPS = 4
KD = 2
NB = NV + NC
PAIRS = STEPS * KD * KD
MESH = pl.DeviceIdType.MESH
F32 = jnp.float32
BF16 = jnp.bfloat16
I32 = jnp.int32


def plane_table(points):
    indices = np.arange(points, dtype=np.int64)
    phase_index = (2 * indices[:, None] + 1) * (2 * indices[None, :] + 1) % (8 * points)
    angles = phase_index * (math.pi / (4 * points))
    return (np.cos(angles) * math.sqrt(2.0 / points)).astype(np.float32).astype(ml_dtypes.bfloat16)


def dot_nn(a, b):
    return lax.dot_general(a, b, (((1,), (0,)), ((), ())), preferred_element_type=F32)


def dot_nt(a, b):
    return lax.dot_general(a, b, (((1,), (1,)), ((), ())), preferred_element_type=F32)


def iota(shape, dim):
    return lax.broadcasted_iota(I32, shape, dim)


def split_dot(value, table):
    rows = value.shape[0]
    high = value.astype(BF16)
    low = (value - high.astype(F32)).astype(BF16)
    both = dot_nn(jnp.concatenate([high, low], axis=0), table)
    return both[:rows] + both[rows:]


def split_grid(ids):
    row = (ids * 43691) >> 21
    return row, ids - row * NKY


def kernel_body(
    n_grp, n_blk, ids_ref, band_hbm, screened_hbm, coulomb_hbm, umklapp_hbm, planes_hbm,
    out_ref, mirror_ref,
    band, screened, coulomb, umklapp, planes,
    id_send, id_recv, q_slots, w_send, w_recv, band_recv,
    products, densities, weighted, screen, shuffle_d, shuffle_e, shuffle_m, m_send, m_recv,
    local_sem, id_ss, id_rs, q_ss, q_rs, w_ss, w_rs, b_ss, b_rs, m_ss, m_rs,
):
    grp = lax.axis_index("grp")
    blk = lax.axis_index("blk")
    points = planes.shape[1]
    owned = screened.shape[0]

    locals_ = [
        pltpu.make_async_copy(src, dst, local_sem.at[n])
        for n, (src, dst) in enumerate(
            [
                (band_hbm, band),
                (screened_hbm, screened),
                (planes_hbm, planes),
                (umklapp_hbm, umklapp),
                (coulomb_hbm, coulomb),
            ]
        )
    ]
    for copy in locals_:
        copy.start()

    def blk_dev(offset):
        return (grp, lax.rem(blk + offset + n_blk, n_blk))

    def grp_dev(offset):
        return (lax.rem(grp + offset + n_grp, n_grp), blk)

    barrier = pltpu.get_barrier_semaphore()
    offsets = sorted({s % n_blk for s in range(1, STEPS + 1)} | {-s % n_blk for s in range(1, STEPS + 1)})
    for offset in offsets:
        pl.semaphore_signal(barrier, inc=1, device_id=blk_dev(offset), device_id_type=MESH)
    for offset in range(1, n_grp):
        pl.semaphore_signal(barrier, inc=1, device_id=grp_dev(offset), device_id_type=MESH)

    sub = iota((8, 128), 0)
    id0 = ids_ref[0]
    id1 = ids_ref[1]
    id_send[...] = jnp.where((sub & 2) == 0, id0, id1)
    own_row, own_col = split_grid(jnp.where((sub & 1) == 0, id0, id1))

    pl.semaphore_wait(barrier, len(offsets) + n_grp - 1)

    id_copies = []
    for s in range(STEPS):
        copy = pltpu.make_async_remote_copy(
            id_send, id_recv.at[s], id_ss.at[s], id_rs.at[s],
            device_id=blk_dev(s + 1), device_id_type=MESH,
        )
        copy.start()
        id_copies.append(copy)
    band_copies = []
    for s in range(STEPS):
        copy = pltpu.make_async_remote_copy(
            band_hbm, band_recv.at[s], b_ss.at[s], b_rs.at[s],
            device_id=blk_dev(s + 1), device_id_type=MESH,
        )
        copy.start()
        band_copies.append(copy)

    col = iota((PAIRS * 16, 256), 0) & 15
    lane = iota((PAIRS * 16, 256), 1)
    shuffle_d[...] = jnp.where(col == (lane >> 6) * 4 + ((lane >> 2) & 3), 1.0, 0.0).astype(BF16)
    shuffle_e[...] = jnp.where(col[:128] == (lane[:128] & 15), 1.0, 0.0).astype(BF16)
    shuffle_m[...] = jnp.where(
        iota((256, 256), 0) == ((lane & 15) << 4) + (lane >> 4), 1.0, 0.0
    ).astype(BF16)

    for copy in id_copies:
        copy.wait_recv()
    class_tiles = []
    for t in range(2):
        other = jnp.where(sub < 4, id_recv[2 * t], id_recv[2 * t + 1])
        row, column = split_grid(other)
        d_row = own_row - row
        d_col = own_col - column
        momentum = jnp.where(d_row < 0, d_row + NKX, d_row) * NKY + jnp.where(
            d_col < 0, d_col + NKY, d_col
        )
        q_slots[0, 8 * t : 8 * t + 8] = momentum
        class_tiles.append(
            jnp.where(d_row < 0, 1, 0) + jnp.where(d_col < 0, 2, 0)
        )
    q_copies = []
    for t in range(1, n_grp):
        copy = pltpu.make_async_remote_copy(
            q_slots.at[0], q_slots.at[t], q_ss.at[t], q_rs.at[t],
            device_id=grp_dev(t), device_id_type=MESH,
        )
        copy.start()
        q_copies.append(copy)

    locals_[0].wait()

    def tiles_of(states):
        x = states.astype(F32)
        y = pltpu.roll(x, 4, 0)
        low = iota(x.shape, 0) < 4
        return jnp.where(low, x, y), jnp.where(low, y, x)

    def repeated(states, first):
        x = states.astype(F32)
        low = iota(x.shape, 0) < 4
        return [
            jnp.where(low, x[first + 2 * h : first + 2 * h + 1], x[first + 2 * h + 1 : first + 2 * h + 2])
            for h in range(2)
        ]

    def store_products(row, rep, tiled):
        products[row : row + 16] = jnp.concatenate(
            [(rep[0] * tiled), (rep[1] * tiled)], axis=0
        ).astype(BF16)

    n_rho = PAIRS * 16
    pair_row = 2 * n_rho
    own_row0 = pair_row + STEPS * KD * 16
    own = [band[i] for i in range(KD)]
    for i in range(KD):
        _, tiled_c = tiles_of(own[i])
        store_products(own_row0 + 16 * i, repeated(own[i], 0), tiled_c)

    for copy in q_copies:
        copy.wait_recv()
    locals_[1].wait()
    wanted = q_slots[...].reshape(n_grp * 16, 128)[:, :1] - grp * owned
    one_hot = jnp.where(
        jnp.broadcast_to(wanted, (n_grp * 16, owned)) == iota((n_grp * 16, owned), 1), 1.0, 0.0
    ).astype(BF16)
    w_send[...] = dot_nn(one_hot, screened[...]).astype(BF16).reshape(n_grp, 16, points)
    w_copies = []
    for t in range(1, n_grp):
        copy = pltpu.make_async_remote_copy(
            w_send.at[t], w_recv.at[t], w_ss.at[t], w_rs.at[t],
            device_id=grp_dev(-t), device_id_type=MESH,
        )
        copy.start()
        w_copies.append(copy)

    for s in range(STEPS):
        band_copies[s].wait_recv()
        for j in range(KD):
            other = band_recv[s, j]
            tiled_v, tiled_c = tiles_of(other)
            store_products(pair_row + (s * KD + j) * 16, repeated(other, 0), tiled_c)
            for i in range(KD):
                p = (s * KD + j) * KD + i
                store_products(p * 16, repeated(own[i], NV), tiled_c)
                store_products(n_rho + p * 16, repeated(own[i], 0), tiled_v)

    locals_[2].wait()
    densities[...] = dot_nn(products[...], planes[...]).astype(BF16)

    locals_[4].wait()
    own_x = (densities[own_row0 : own_row0 + 32].astype(F32) * coulomb[...]).astype(BF16)
    exchange = dot_nt(own_x, densities[pair_row : pair_row + STEPS * KD * 16])
    spread = jnp.concatenate([exchange] * (STEPS * KD), axis=0)
    spread = jnp.where(
        (iota(spread.shape, 0) >> 5) == (iota(spread.shape, 1) >> 4), spread, 0.0
    )
    spread_x = split_dot(spread, shuffle_e[...])
    mrow = iota((n_rho, 256), 0) & 15
    mlane = iota((n_rho, 256), 1)
    total_x = jnp.where(mrow == (mlane >> 4), 2.0 * spread_x, 0.0)

    locals_[3].wait()
    for copy in w_copies:
        copy.wait_recv()
    for t in range(2):
        rows = pl.ds(8 * t, 8)
        got = w_send[0].astype(F32)[8 * t : 8 * t + 8]
        for g in range(1, n_grp):
            got = got + w_recv[g].astype(F32)[8 * t : 8 * t + 8]
        shift = class_tiles[t]
        for o in range(points // 128):
            lanes = slice(o * 128, o * 128 + 128)
            index = jnp.where(
                shift < 2,
                jnp.where(shift == 0, umklapp[0:1, lanes], umklapp[1:2, lanes]),
                jnp.where(shift == 2, umklapp[2:3, lanes], umklapp[3:4, lanes]),
            )
            inner = index & 127
            outer = index >> 7
            acc = jnp.zeros((8, 128), F32)
            for c in range(points // 128):
                part = jnp.take_along_axis(
                    got[:, c * 128 : c * 128 + 128], inner, axis=1, mode="promise_in_bounds"
                )
                acc = jnp.where(outer == c, part, acc)
            screen[rows, lanes] = acc

    for p in range(PAIRS):
        weighted[p * 16 : p * 16 + 16] = (
            densities[p * 16 : p * 16 + 16].astype(F32) * screen[p : p + 1]
        ).astype(BF16)
    direct = dot_nt(weighted[...], densities[n_rho : 2 * n_rho])
    direct = jnp.where((iota(direct.shape, 0) >> 4) == (iota(direct.shape, 1) >> 4), direct, 0.0)
    spread_d = split_dot(direct, shuffle_d[...])
    total = total_x - jnp.where(
        mrow == ((mlane >> 4) & 3) * 4 + (mlane & 3), spread_d, 0.0
    )
    total = total.reshape(PAIRS, 16, 256).sum(axis=1) * (1.0 / math.sqrt(points))
    turned = split_dot(total, shuffle_m[...])

    m_copies = []
    for s in range(STEPS):
        for j in range(KD):
            for i in range(KD):
                p = (s * KD + j) * KD + i
                m_send[s, j : j + 1, i * 256 : i * 256 + 256] = turned[p : p + 1]
        copy = pltpu.make_async_remote_copy(
            m_send.at[s], m_recv.at[s], m_ss.at[s], m_rs.at[s],
            device_id=blk_dev(-(s + 1)), device_id_type=MESH,
        )
        copy.start()
        m_copies.append(copy)
    for s in range(STEPS):
        for j in range(KD):
            for i in range(KD):
                p = (s * KD + j) * KD + i
                out_ref[i, s : s + 1, j * 256 : j * 256 + 256] = total[p : p + 1]
    for copy in id_copies + q_copies + w_copies + band_copies:
        copy.wait_send()
    for s in range(STEPS):
        m_copies[s].wait_recv()
        for k in range(KD):
            mirror_ref[k, s : s + 1] = m_recv[s, k : k + 1]
    for copy in m_copies:
        copy.wait_send()


def per_device(n_grp, n_blk, band_states, kpoint_ids, screened, coulomb, umklapp_map):
    points = band_states.shape[2]
    owned = screened.shape[0]
    rows = 2 * PAIRS * 16 + STEPS * KD * 16 + KD * 16
    planes = jnp.asarray(plane_table(points))
    any_spec = pl.BlockSpec(memory_space=pl.ANY)
    dma = pltpu.SemaphoreType.DMA
    shape = jax.ShapeDtypeStruct((KD, STEPS, KD * 256), F32)
    return pl.pallas_call(
        functools.partial(kernel_body, n_grp, n_blk),
        out_shape=(shape, shape),
        in_specs=[pl.BlockSpec(memory_space=pltpu.SMEM)] + [any_spec] * 5,
        out_specs=(pl.BlockSpec(memory_space=pltpu.VMEM),) * 2,
        scratch_shapes=[
            pltpu.VMEM((KD, NB, points), BF16),
            pltpu.VMEM((owned, points), BF16),
            pltpu.VMEM((1, points), F32),
            pltpu.VMEM((4, points), I32),
            pltpu.VMEM((points, points), BF16),
            pltpu.VMEM((8, 128), I32),
            pltpu.VMEM((STEPS, 8, 128), I32),
            pltpu.VMEM((n_grp, 16, 128), I32),
            pltpu.VMEM((n_grp, 16, points), BF16),
            pltpu.VMEM((n_grp, 16, points), BF16),
            pltpu.VMEM((STEPS, KD, NB, points), BF16),
            pltpu.VMEM((rows, points), BF16),
            pltpu.VMEM((rows, points), BF16),
            pltpu.VMEM((PAIRS * 16, points), BF16),
            pltpu.VMEM((16, points), F32),
            pltpu.VMEM((256, 256), BF16),
            pltpu.VMEM((128, 256), BF16),
            pltpu.VMEM((256, 256), BF16),
            pltpu.VMEM((STEPS, KD, 512), F32),
            pltpu.VMEM((STEPS, KD, 512), F32),
            dma((5,)),
            dma((STEPS,)), dma((STEPS,)),
            dma((n_grp,)), dma((n_grp,)),
            dma((n_grp,)), dma((n_grp,)),
            dma((STEPS,)), dma((STEPS,)),
            dma((STEPS,)), dma((STEPS,)),
        ],
        compiler_params=pltpu.CompilerParams(
            collective_id=0, has_side_effects=True, vmem_limit_bytes=40 * 2**20
        ),
    )(kpoint_ids, band_states, screened, coulomb.reshape(1, points), umklapp_map, planes)


def solution(mesh):
    return jax.shard_map(
        functools.partial(per_device, mesh.shape["grp"], mesh.shape["blk"]),
        mesh=mesh,
        in_specs=(P(("grp", "blk"), None, None), P(("grp", "blk")), P("grp", None), P(), P()),
        out_specs=(P(("grp", "blk"), None, None), P(("grp", "blk"), None, None)),
        check_vma=False,
    )
```

profile of v0, /device:TPU:0, one launch (start us, length us, event | category | flops | bytes accessed | tf_op | source)
XLA Modules:
  0.0 30.6 jit_solution(15353686829775711834)
XLA Ops:
  0.6 0.7 %reshape.7.coulomb_hbm = f32[1,1152]{1,0:T(1,128)S(1)} reshape(f32[1152]{0:T(1024)} %param.9) | data formatting | bytes 9216 | tf_op jit(solution)/shard_map/reshape | solution.py:339
  1.3 0.0 copy-start
  1.3 1.7 %copy-done = bf16[1152,1152]{1,0:T(8,128)(2,1)S(1)} copy-done((bf16[1152,1152]{1,0:T(8,128)(2,1)S(1)}, bf16[1152,1152]{1,0:T(8,128)(2,1)}, u32[]{:S(2)}) %copy-start) | copy-done | bytes 2654232
  3.1 0.0 copy-start.1
  3.1 1.3 %copy-done.1 = bf16[576,1152]{1,0:T(8,128)(2,1)S(1)} copy-done((bf16[576,1152]{1,0:T(8,128)(2,1)S(1)}, bf16[576,1152]{1,0:T(8,128)(2,1)}, u32[]{:S(2)}) %copy-start.1) | copy-done | bytes 1327128
  4.4 0.0 copy-start.2
  4.4 0.8 %copy-done.2 = bf16[2,8,1152]{2,1,0:T(8,128)(2,1)S(1)} copy-done((bf16[2,8,1152]{2,1,0:T(8,128)(2,1)S(1)}, bf16[2,8,1152]{2,1,0:T(8,128)(2,1)}, u32[]{:S(2)}) %copy-start.2) | copy-done | bytes 36888
  5.2 0.0 copy-start.3
  5.2 0.7 %copy-done.3 = s32[4,1152]{1,0:T(4,128)S(1)} copy-done((s32[4,1152]{1,0:T(4,128)S(1)}, s32[4,1152]{1,0:T(4,128)}, u32[]{:S(2)}) %copy-start.3) | copy-done | bytes 18456
  5.9 0.0 copy-start.4
  5.9 0.7 %copy-done.4 = s32[2]{0:T(128)S(1)} copy-done((s32[2]{0:T(128)S(1)}, s32[2]{0:T(128)}, u32[]{:S(2)}) %copy-start.4) | copy-done | bytes 32
  6.6 22.8 %shard_map.77 = (f32[2,4,512]{2,1,0:T(4,128)S(1)}, f32[2,4,512]{2,1,0:T(4,128)S(1)}) custom-call(s32[2]{0:T(128)S(1)} %copy-done.4, bf16[2,8,1152]{2,1,0:T(8,128)(2,1)S(1)} %copy-done.2, bf16[576,1152]{1,0:T(8,128)(2,1)S(1)} %copy-done.1, f32[1,1152]{1,0:T(1,128)S(1)} %reshape.7.coulomb_hbm, s32[4,1152]{1,0:T(4,128)S(1)} %copy-done.3, ...), custom_call_target="tpu_custom_call" | custom-call | tf_op jit(solution)/shard_map/pallas_call | solution.py:303
  29.4 0.6 %copy.10 = f32[2,4,512]{2,1,0:T(4,128)} copy(f32[2,4,512]{2,1,0:T(4,128)S(1)} %get-tuple-element.4) | data formatting | bytes 32768
  30.0 0.6 %copy.11 = f32[2,4,512]{2,1,0:T(4,128)} copy(f32[2,4,512]{2,1,0:T(4,128)S(1)} %get-tuple-element.5) | data formatting | bytes 32768
Async XLA Ops:
  1.3 1.7 %copy-start = (bf16[1152,1152]{1,0:T(8,128)(2,1)S(1)}, bf16[1152,1152]{1,0:T(8,128)(2,1)}, u32[]{:S(2)}) copy-start(bf16[1152,1152]{1,0:T(8,128)(2,1)} %constant.2.clone.planes_hbm) | copy-start | bytes 7962628
  3.1 1.3 %copy-start.1 = (bf16[576,1152]{1,0:T(8,128)(2,1)S(1)}, bf16[576,1152]{1,0:T(8,128)(2,1)}, u32[]{:S(2)}) copy-start(bf16[576,1152]{1,0:T(8,128)(2,1)} %screened_hbm.1) | copy-start | bytes 3981316
  4.4 0.8 %copy-start.2 = (bf16[2,8,1152]{2,1,0:T(8,128)(2,1)S(1)}, bf16[2,8,1152]{2,1,0:T(8,128)(2,1)}, u32[]{:S(2)}) copy-start(bf16[2,8,1152]{2,1,0:T(8,128)(2,1)} %band_hbm.1) | copy-start | bytes 110596
  5.2 0.7 %copy-start.3 = (s32[4,1152]{1,0:T(4,128)S(1)}, s32[4,1152]{1,0:T(4,128)}, u32[]{:S(2)}) copy-start(s32[4,1152]{1,0:T(4,128)} %umklapp_hbm.1) | copy-start | bytes 55300
  5.9 0.7 %copy-start.4 = (s32[2]{0:T(128)S(1)}, s32[2]{0:T(128)}, u32[]{:S(2)}) copy-start(s32[2]{0:T(128)} %ids_ref.1) | copy-start | bytes 28
where the time goes:
time: 30.9 us; the launch traced here: 30.6 us
  Pallas kernels  22.8 us (74%)
  local copies, waits for them, and re-layouts  7.13 us (23%)
  between operations  0.64 us (2%)
    pallas_call x1, Pallas kernels, per_device(): pl.pallas_call(functools.partial(kernel_body, n_grp, n_blk), out_shape=(s...  22.8 us
    unnamed x12, local copies, waits for them, and re-layouts  6.43 us
    reshape x1, local copies, waits for them, and re-layouts, per_device(): coulomb.reshape(1, points)  0.7 us

commit v1 on v0

--- a/solution.py
+++ b/solution.py
@@ -61,7 +61,7 @@
     out_ref, mirror_ref,
     band, screened, coulomb, umklapp, planes,
     id_send, id_recv, q_slots, w_send, w_recv, band_recv,
-    products, densities, weighted, screen, shuffle_d, shuffle_e, shuffle_m, m_send, m_recv,
+    products, densities, weighted, screen, shuffle_d, shuffle_e, shuffle_m, m_send, rows_out,
     local_sem, id_ss, id_rs, q_ss, q_rs, w_ss, w_rs, b_ss, b_rs, m_ss, m_rs,
 ):
     grp = lax.axis_index("grp")
@@ -113,15 +113,6 @@
         )
         copy.start()
         id_copies.append(copy)
-    band_copies = []
-    for s in range(STEPS):
-        copy = pltpu.make_async_remote_copy(
-            band_hbm, band_recv.at[s], b_ss.at[s], b_rs.at[s],
-            device_id=blk_dev(s + 1), device_id_type=MESH,
-        )
-        copy.start()
-        band_copies.append(copy)
-
     col = iota((PAIRS * 16, 256), 0) & 15
     lane = iota((PAIRS * 16, 256), 1)
     shuffle_d[...] = jnp.where(col == (lane >> 6) * 4 + ((lane >> 2) & 3), 1.0, 0.0).astype(BF16)
@@ -154,6 +145,15 @@
         copy.start()
         q_copies.append(copy)
 
+    band_copies = []
+    for s in range(STEPS):
+        copy = pltpu.make_async_remote_copy(
+            band_hbm, band_recv.at[s], b_ss.at[s], b_rs.at[s],
+            device_id=blk_dev(s + 1), device_id_type=MESH,
+        )
+        copy.start()
+        band_copies.append(copy)
+
     locals_[0].wait()
 
     def tiles_of(states):
@@ -186,19 +186,22 @@
     for copy in q_copies:
         copy.wait_recv()
     locals_[1].wait()
-    wanted = q_slots[...].reshape(n_grp * 16, 128)[:, :1] - grp * owned
+    wanted = jnp.concatenate(
+        [q_slots[t, 8 * h : 8 * h + 8] for h in range(2) for t in range(n_grp)], axis=0
+    )[:, :1] - grp * owned
     one_hot = jnp.where(
         jnp.broadcast_to(wanted, (n_grp * 16, owned)) == iota((n_grp * 16, owned), 1), 1.0, 0.0
     ).astype(BF16)
-    w_send[...] = dot_nn(one_hot, screened[...]).astype(BF16).reshape(n_grp, 16, points)
-    w_copies = []
-    for t in range(1, n_grp):
-        copy = pltpu.make_async_remote_copy(
-            w_send.at[t], w_recv.at[t], w_ss.at[t], w_rs.at[t],
-            device_id=grp_dev(-t), device_id_type=MESH,
-        )
-        copy.start()
-        w_copies.append(copy)
+    w_send[...] = dot_nn(one_hot, screened[...]).reshape(2, n_grp, 8, points).astype(BF16)
+    w_copies = [[], []]
+    for h in range(2):
+        for t in range(1, n_grp):
+            copy = pltpu.make_async_remote_copy(
+                w_send.at[h, t], w_recv.at[h, t], w_ss.at[h, t], w_rs.at[h, t],
+                device_id=grp_dev(-t), device_id_type=MESH,
+            )
+            copy.start()
+            w_copies[h].append(copy)
 
     for s in range(STEPS):
         band_copies[s].wait_recv()
@@ -215,26 +218,29 @@
     densities[...] = dot_nn(products[...], planes[...]).astype(BF16)
 
     locals_[4].wait()
-    own_x = (densities[own_row0 : own_row0 + 32].astype(F32) * coulomb[...]).astype(BF16)
+    own_x = (densities[own_row0 : own_row0 + 32].astype(F32) * coulomb[...].reshape(1, points)).astype(BF16)
     exchange = dot_nt(own_x, densities[pair_row : pair_row + STEPS * KD * 16])
     spread = jnp.concatenate([exchange] * (STEPS * KD), axis=0)
     spread = jnp.where(
         (iota(spread.shape, 0) >> 5) == (iota(spread.shape, 1) >> 4), spread, 0.0
     )
     spread_x = split_dot(spread, shuffle_e[...])
-    mrow = iota((n_rho, 256), 0) & 15
-    mlane = iota((n_rho, 256), 1)
-    total_x = jnp.where(mrow == (mlane >> 4), 2.0 * spread_x, 0.0)
+    half = n_rho // 2
+    mrow = iota((half, 256), 0) & 15
+    mlane = iota((half, 256), 1)
+    keep_x = mrow == (mlane >> 4)
+    keep_d = mrow == ((mlane >> 4) & 3) * 4 + (mlane & 3)
+    diagonal = (iota((half, half), 0) >> 4) == (iota((half, half), 1) >> 4)
+    total_x = [
+        jnp.where(keep_x, 2.0 * spread_x[h * half : h * half + half], 0.0) for h in range(2)
+    ]
 
     locals_[3].wait()
-    for copy in w_copies:
-        copy.wait_recv()
-    for t in range(2):
-        rows = pl.ds(8 * t, 8)
-        got = w_send[0].astype(F32)[8 * t : 8 * t + 8]
-        for g in range(1, n_grp):
-            got = got + w_recv[g].astype(F32)[8 * t : 8 * t + 8]
-        shift = class_tiles[t]
+    m_copies = []
+    for h in range(2):
+        shift = class_tiles[h]
+        inner = []
+        outer = []
         for o in range(points // 128):
             lanes = slice(o * 128, o * 128 + 128)
             index = jnp.where(
@@ -242,54 +248,66 @@
                 jnp.where(shift == 0, umklapp[0:1, lanes], umklapp[1:2, lanes]),
                 jnp.where(shift == 2, umklapp[2:3, lanes], umklapp[3:4, lanes]),
             )
-            inner = index & 127
-            outer = index >> 7
+            inner.append(index & 127)
+            outer.append(index >> 7)
+        for copy in w_copies[h]:
+            copy.wait_recv()
+        got = w_send[h, 0].astype(F32)
+        for g in range(1, n_grp):
+            got = got + w_recv[h, g].astype(F32)
+        for o in range(points // 128):
             acc = jnp.zeros((8, 128), F32)
             for c in range(points // 128):
                 part = jnp.take_along_axis(
-                    got[:, c * 128 : c * 128 + 128], inner, axis=1, mode="promise_in_bounds"
+                    got[:, c * 128 : c * 128 + 128], inner[o], axis=1, mode="promise_in_bounds"
                 )
-                acc = jnp.where(outer == c, part, acc)
-            screen[rows, lanes] = acc
-
-    for p in range(PAIRS):
-        weighted[p * 16 : p * 16 + 16] = (
-            densities[p * 16 : p * 16 + 16].astype(F32) * screen[p : p + 1]
-        ).astype(BF16)
-    direct = dot_nt(weighted[...], densities[n_rho : 2 * n_rho])
-    direct = jnp.where((iota(direct.shape, 0) >> 4) == (iota(direct.shape, 1) >> 4), direct, 0.0)
-    spread_d = split_dot(direct, shuffle_d[...])
-    total = total_x - jnp.where(
-        mrow == ((mlane >> 4) & 3) * 4 + (mlane & 3), spread_d, 0.0
-    )
-    total = total.reshape(PAIRS, 16, 256).sum(axis=1) * (1.0 / math.sqrt(points))
-    turned = split_dot(total, shuffle_m[...])
-
-    m_copies = []
-    for s in range(STEPS):
-        for j in range(KD):
-            for i in range(KD):
-                p = (s * KD + j) * KD + i
-                m_send[s, j : j + 1, i * 256 : i * 256 + 256] = turned[p : p + 1]
-        copy = pltpu.make_async_remote_copy(
-            m_send.at[s], m_recv.at[s], m_ss.at[s], m_rs.at[s],
-            device_id=blk_dev(-(s + 1)), device_id_type=MESH,
-        )
-        copy.start()
-        m_copies.append(copy)
-    for s in range(STEPS):
-        for j in range(KD):
-            for i in range(KD):
-                p = (s * KD + j) * KD + i
-                out_ref[i, s : s + 1, j * 256 : j * 256 + 256] = total[p : p + 1]
-    for copy in id_copies + q_copies + w_copies + band_copies:
+                acc = jnp.where(outer[o] == c, part, acc)
+            screen[8 * h : 8 * h + 8, o * 128 : o * 128 + 128] = acc
+
+        first = h * half
+        for p in range(8 * h, 8 * h + 8):
+            weighted[p * 16 : p * 16 + 16] = (
+                densities[p * 16 : p * 16 + 16].astype(F32) * screen[p : p + 1]
+            ).astype(BF16)
+        direct = dot_nt(
+            weighted[first : first + half], densities[n_rho + first : n_rho + first + half]
+        )
+        spread_d = split_dot(jnp.where(diagonal, direct, 0.0), shuffle_d[:half])
+        total = total_x[h] - jnp.where(keep_d, spread_d, 0.0)
+        total = total.reshape(8, 16, 256).sum(axis=1) * (1.0 / math.sqrt(points))
+        turned = split_dot(total, shuffle_m[...])
+        for s in (2 * h, 2 * h + 1):
+            for j in range(KD):
+                for i in range(KD):
+                    p = (s * KD + j) * KD + i - 8 * h
+                    m_send[s, j : j + 1, i * 256 : i * 256 + 256] = turned[p : p + 1]
+            copy = pltpu.make_async_remote_copy(
+                m_send.at[s], mirror_ref.at[s], m_ss.at[s], m_rs.at[s],
+                device_id=blk_dev(-(s + 1)), device_id_type=MESH,
+            )
+            copy.start()
+            m_copies.append(copy)
+        for s in (2 * h, 2 * h + 1):
+            for j in range(KD):
+                for i in range(KD):
+                    p = (s * KD + j) * KD + i - 8 * h
+                    rows_out[i, s : s + 1, j * 256 : j * 256 + 256] = total[p : p + 1]
+    out_copy = pltpu.make_async_copy(rows_out, out_ref, local_sem.at[5])
+    out_copy.start()
+    for copy in id_copies + q_copies + w_copies[0] + w_copies[1] + band_copies:
         copy.wait_send()
-    for s in range(STEPS):
-        m_copies[s].wait_recv()
-        for k in range(KD):
-            mirror_ref[k, s : s + 1] = m_recv[s, k : k + 1]
+    for copy in m_copies:
+        copy.wait_recv()
+    out_copy.wait()
     for copy in m_copies:
         copy.wait_send()
+
+
+def finish_body(blocks, turned, out_ref, mirror_ref):
+    out_ref[...] = blocks[...]
+    for s in range(STEPS):
+        for k in range(KD):
+            mirror_ref[k, s : s + 1] = turned[s, k : k + 1]
 
 
 def per_device(n_grp, n_blk, band_states, kpoint_ids, screened, coulomb, umklapp_map):
@@ -297,25 +315,26 @@
     owned = screened.shape[0]
     rows = 2 * PAIRS * 16 + STEPS * KD * 16 + KD * 16
     planes = jnp.asarray(plane_table(points))
-    any_spec = pl.BlockSpec(memory_space=pl.ANY)
+    any_spec = pl.BlockSpec(memory_space=pltpu.HBM)
     dma = pltpu.SemaphoreType.DMA
     shape = jax.ShapeDtypeStruct((KD, STEPS, KD * 256), F32)
-    return pl.pallas_call(
+    arrived = jax.ShapeDtypeStruct((STEPS, KD, KD * 256), F32)
+    blocks, turned = pl.pallas_call(
         functools.partial(kernel_body, n_grp, n_blk),
-        out_shape=(shape, shape),
+        out_shape=(shape, arrived),
         in_specs=[pl.BlockSpec(memory_space=pltpu.SMEM)] + [any_spec] * 5,
-        out_specs=(pl.BlockSpec(memory_space=pltpu.VMEM),) * 2,
+        out_specs=(any_spec,) * 2,
         scratch_shapes=[
             pltpu.VMEM((KD, NB, points), BF16),
             pltpu.VMEM((owned, points), BF16),
-            pltpu.VMEM((1, points), F32),
+            pltpu.VMEM((points,), F32),
             pltpu.VMEM((4, points), I32),
             pltpu.VMEM((points, points), BF16),
             pltpu.VMEM((8, 128), I32),
             pltpu.VMEM((STEPS, 8, 128), I32),
             pltpu.VMEM((n_grp, 16, 128), I32),
-            pltpu.VMEM((n_grp, 16, points), BF16),
-            pltpu.VMEM((n_grp, 16, points), BF16),
+            pltpu.VMEM((2, n_grp, 8, points), BF16),
+            pltpu.VMEM((2, n_grp, 8, points), BF16),
             pltpu.VMEM((STEPS, KD, NB, points), BF16),
             pltpu.VMEM((rows, points), BF16),
             pltpu.VMEM((rows, points), BF16),
@@ -325,18 +344,25 @@
             pltpu.VMEM((128, 256), BF16),
             pltpu.VMEM((256, 256), BF16),
             pltpu.VMEM((STEPS, KD, 512), F32),
-            pltpu.VMEM((STEPS, KD, 512), F32),
-            dma((5,)),
+            pltpu.VMEM((KD, STEPS, 512), F32),
+            dma((6,)),
             dma((STEPS,)), dma((STEPS,)),
             dma((n_grp,)), dma((n_grp,)),
-            dma((n_grp,)), dma((n_grp,)),
+            dma((2, n_grp)), dma((2, n_grp)),
             dma((STEPS,)), dma((STEPS,)),
             dma((STEPS,)), dma((STEPS,)),
         ],
         compiler_params=pltpu.CompilerParams(
-            collective_id=0, has_side_effects=True, vmem_limit_bytes=40 * 2**20
+            collective_id=0, has_side_effects=True, vmem_limit_bytes=63 * 2**20
         ),
-    )(kpoint_ids, band_states, screened, coulomb.reshape(1, points), umklapp_map, planes)
+    )(kpoint_ids, band_states, screened, coulomb, umklapp_map, planes)
+    return pl.pallas_call(
+        finish_body,
+        out_shape=(shape, shape),
+        in_specs=[pl.BlockSpec(memory_space=pltpu.VMEM)] * 2,
+        out_specs=(pl.BlockSpec(memory_space=pltpu.VMEM),) * 2,
+        compiler_params=pltpu.CompilerParams(vmem_limit_bytes=63 * 2**20),
+    )(blocks, turned)
 
 
 def solution(mesh):

time: 30.9 us -> 24.8 us (0.80)
  local copies, waits for them, and re-layouts: 7.13 us -> 0 us
  Pallas kernels: 22.8 us -> 23.9 us
    unnamed x12 -> x0, local copies, waits for them, and re-layouts: 6.43 us -> none
    pallas_call x0 -> x1, Pallas kernels: none -> 1.35 us  [per_device(): pl.pallas_call(finish_body, out_shape=(shape, shape), in_specs=[pl.BlockS...]
    reshape x1 -> x0, local copies, waits for them, and re-layouts: 0.7 us -> none  [per_device(): coulomb.reshape(1, points)]
where the time goes in v1:
time: 24.8 us; the launch traced here: 24.5 us
  Pallas kernels  23.9 us (96%)
  between operations  0.64 us (3%)
    pallas_call x1, Pallas kernels, per_device(): pl.pallas_call(functools.partial(kernel_body, n_grp, n_blk), out_shape=(s...  22.5 us
    pallas_call x1, Pallas kernels, per_device(): pl.pallas_call(finish_body, out_shape=(shape, shape), in_specs=[pl.BlockS...  1.35 us

profile of v1, /device:TPU:0, one launch (start us, length us, event | category | flops | bytes accessed | tf_op | source)
XLA Modules:
  0.0 24.5 jit_solution(1716587041954186372)
XLA Ops:
  0.6 22.5 %shard_map.77 = (f32[2,4,512]{2,1,0:T(4,128)}, f32[4,2,512]{2,1,0:T(2,128)}) custom-call(s32[2]{0:T(128)} %ids_ref.1, bf16[2,8,1152]{2,1,0:T(8,128)(2,1)} %band_hbm.1, bf16[576,1152]{1,0:T(8,128)(2,1)} %screened_hbm.1, f32[1152]{0:T(1024)} %coulomb_hbm.1, s32[4,1152]{1,0:T(4,128)} %umklapp_hbm.1, bf16[1152,1152]{1,0:T(8,128)(2,1)} %constant.2.clone.planes_hbm), custom_call_target="tpu_custom_call" | custom-call | tf_op jit(solution)/shard_map/pallas_call | solution.py:322
  23.2 1.4 %shard_map.78 = (f32[2,4,512]{2,1,0:T(4,128)}, f32[2,4,512]{2,1,0:T(4,128)}) custom-call(f32[2,4,512]{2,1,0:T(4,128)} %get-tuple-element.4.blocks, f32[4,2,512]{2,1,0:T(2,128)} %get-tuple-element.5.turned), custom_call_target="tpu_custom_call" | custom-call | tf_op jit(solution)/shard_map/pallas_call | solution.py:359

commit v2 on v1

--- a/solution.py
+++ b/solution.py
@@ -57,9 +57,9 @@
 
 
 def kernel_body(
-    n_grp, n_blk, ids_ref, band_hbm, screened_hbm, coulomb_hbm, umklapp_hbm, planes_hbm,
+    n_grp, n_blk, ids_hbm, band_hbm, screened_hbm, coulomb_hbm, umklapp_hbm, planes_hbm,
     out_ref, mirror_ref,
-    band, screened, coulomb, umklapp, planes,
+    ids_ref, band, screened, coulomb, umklapp, planes,
     id_send, id_recv, q_slots, w_send, w_recv, band_recv,
     products, densities, weighted, screen, shuffle_d, shuffle_e, shuffle_m, m_send, rows_out,
     local_sem, id_ss, id_rs, q_ss, q_rs, w_ss, w_rs, b_ss, b_rs, m_ss, m_rs,
@@ -69,6 +69,8 @@
     points = planes.shape[1]
     owned = screened.shape[0]
 
+    ids_copy = pltpu.make_async_copy(ids_hbm, ids_ref, local_sem.at[6])
+    ids_copy.start()
     locals_ = [
         pltpu.make_async_copy(src, dst, local_sem.at[n])
         for n, (src, dst) in enumerate(
@@ -81,8 +83,6 @@
             ]
         )
     ]
-    for copy in locals_:
-        copy.start()
 
     def blk_dev(offset):
         return (grp, lax.rem(blk + offset + n_blk, n_blk))
@@ -97,7 +97,10 @@
     for offset in range(1, n_grp):
         pl.semaphore_signal(barrier, inc=1, device_id=grp_dev(offset), device_id_type=MESH)
 
+    for copy in locals_:
+        copy.start()
     sub = iota((8, 128), 0)
+    ids_copy.wait()
     id0 = ids_ref[0]
     id1 = ids_ref[1]
     id_send[...] = jnp.where((sub & 2) == 0, id0, id1)
@@ -322,9 +325,10 @@
     blocks, turned = pl.pallas_call(
         functools.partial(kernel_body, n_grp, n_blk),
         out_shape=(shape, arrived),
-        in_specs=[pl.BlockSpec(memory_space=pltpu.SMEM)] + [any_spec] * 5,
+        in_specs=[any_spec] * 6,
         out_specs=(any_spec,) * 2,
         scratch_shapes=[
+            pltpu.SMEM((KD,), I32),
             pltpu.VMEM((KD, NB, points), BF16),
             pltpu.VMEM((owned, points), BF16),
             pltpu.VMEM((points,), F32),
@@ -345,7 +349,7 @@
             pltpu.VMEM((256, 256), BF16),
             pltpu.VMEM((STEPS, KD, 512), F32),
             pltpu.VMEM((KD, STEPS, 512), F32),
-            dma((6,)),
+            dma((7,)),
             dma((STEPS,)), dma((STEPS,)),
             dma((n_grp,)), dma((n_grp,)),
             dma((2, n_grp)), dma((2, n_grp)),

time: 24.8 us -> 24.1 us (0.972)
  Pallas kernels: 23.9 us -> 23.2 us
    pallas_call x1, Pallas kernels: 22.5 us -> 21.9 us  [per_device(): pl.pallas_call(functools.partial(kernel_body, n_grp, n_blk), out_shape=(s...]
where the time goes in v2:
time: 24.1 us; the launch traced here: 23.9 us
  Pallas kernels  23.2 us (96%)
  between operations  0.64 us (3%)
    pallas_call x1, Pallas kernels, per_device(): pl.pallas_call(functools.partial(kernel_body, n_grp, n_blk), out_shape=(s...  21.9 us
    pallas_call x1, Pallas kernels, per_device(): pl.pallas_call(finish_body, out_shape=(shape, shape), in_specs=[pl.BlockS...  1.35 us

profile of v2, /device:TPU:0, one launch (start us, length us, event | category | flops | bytes accessed | tf_op | source)
XLA Modules:
  0.0 23.9 jit_solution(3273123274274018332)
XLA Ops:
  0.6 21.9 %shard_map.77 = (f32[2,4,512]{2,1,0:T(4,128)}, f32[4,2,512]{2,1,0:T(2,128)}) custom-call(s32[2]{0:T(128)} %ids_hbm.1, bf16[2,8,1152]{2,1,0:T(8,128)(2,1)} %band_hbm.1, bf16[576,1152]{1,0:T(8,128)(2,1)} %screened_hbm.1, f32[1152]{0:T(1024)} %coulomb_hbm.1, s32[4,1152]{1,0:T(4,128)} %umklapp_hbm.1, bf16[1152,1152]{1,0:T(8,128)(2,1)} %constant.2.clone.planes_hbm), custom_call_target="tpu_custom_call" | custom-call | tf_op jit(solution)/shard_map/pallas_call | solution.py:325
  22.5 1.4 %shard_map.78 = (f32[2,4,512]{2,1,0:T(4,128)}, f32[2,4,512]{2,1,0:T(4,128)}) custom-call(f32[2,4,512]{2,1,0:T(4,128)} %get-tuple-element.4.blocks, f32[4,2,512]{2,1,0:T(2,128)} %get-tuple-element.5.turned), custom_call_target="tpu_custom_call" | custom-call | tf_op jit(solution)/shard_map/pallas_call | solution.py:363
